TPU v7x, 32 devices: a whole 2x2x4 slice. The times are simulated.
32 devices in a mesh: group: 2 (over y), ctx: 4 (over z), kvh: 2 (over x), sub: 2 (over core).
Axes of the slice: x: 2, y: 2, z: 4, core: 2. Of those that a mesh axis runs over, the one named last changes fastest.
Arguments:
- queries: bfloat16 [64, 128, 8192], P(('group', 'ctx'), 'sub', 'kvh'), parts along dimension 0, may hold values from -128 to 128
- cache_kv: bfloat16 [192, 128, 2048], P(('group', 'ctx'), None, 'kvh'), parts along dimension 0, may hold values from -4 to 4
- cache_scale: float32 [192, 16], P('group', 'kvh'), parts along dimension 0, may hold values from 0.29 to 3.01
- prompt_key_value: bfloat16 [64, 128, 2048], P(('group', 'ctx'), None, 'kvh'), parts along dimension 0, may hold values from -4 to 4
- prompt_scale: float32 [64, 16], P('group', 'kvh'), parts along dimension 0, may hold values from 0.3 to 3
- rand_blocks: int32 [64, 3], P('group'), parts along dimension 0, may hold values from 0 to 95, as said below
Outputs:
- attended: bfloat16 [64, 128, 8192], P(('group', 'ctx'), 'sub', 'kvh'), parts along dimension 0
There are 2 independent parts, one for each index of `group`. A program takes and returns all parts, laid end to end along the dimension named above; each array names one. Nothing has to cross between parts.
Inputs may be any that keep to these rules, and one draw needn't show every extreme that they name: `rand_blocks`: within each aligned run of 8 prompt blocks, the run's entries name blocks of any one aligned range of 24 cache blocks at most 6 times; one and the same range is named exactly 6 times in every run, and each run has another range so named.
All inputs are finite; a program needn't handle non-finite values.
Results may differ from a plain program's by a relative error of at most 0.0051.
Values may be sent and summed in bfloat16 or wider, within the bound.
A program may use at most 64 MiB of HBM per device.

v0:
```python
import math

import jax
import jax.numpy as jnp
from jax import lax
from jax.sharding import PartitionSpec as P

HEAD_SIZE = 128
NG = 2
WIN = 2


def passed_along(block, axis, distance):
    devices = range(lax.axis_size(axis))
    route = [(i - distance, i) for i in devices if i - distance in devices]
    return lax.ppermute(block, axis, route)


def from_root(block, axis, source):
    block = jnp.where(lax.axis_index(axis) == source, block, jnp.zeros_like(block))
    return lax.psum(block, axis)


def body(queries, cache_kv, cache_scale, prompt_key_value, prompt_scale, rand_blocks):
    ctx_count = lax.axis_size("ctx")
    ctx_index = lax.axis_index("ctx")
    sub_index = lax.axis_index("sub")
    local_blocks, row_count, query_width = queries.shape
    cache_blocks, block_rows, kv_width = cache_kv.shape
    head_dim = HEAD_SIZE
    local_heads = kv_width // (2 * head_dim)
    query_groups = query_width // (local_heads * head_dim)
    rand_count = rand_blocks.shape[1]
    capacity = max(2, (local_blocks * rand_count + ctx_count - 1) // ctx_count)
    window_recv = passed_along(prompt_key_value[local_blocks - WIN :], "ctx", 1)
    per_reader = rand_blocks.reshape(ctx_count, local_blocks * rand_count)
    owners = per_reader // cache_blocks
    owner_hot = (
        owners[:, :, None] == jnp.arange(ctx_count, dtype=jnp.int32)[None, None, :]
    ).astype(jnp.int32)
    slot_rank = jnp.sum((jnp.cumsum(owner_hot, axis=1) - 1) * owner_hot, axis=2)
    picked = (
        (owners == ctx_index)[:, :, None]
        & (slot_rank[:, :, None] == jnp.arange(capacity, dtype=jnp.int32)[None, None, :])
    ).astype(jnp.int32)
    local_ids = jnp.sum(picked * (per_reader % cache_blocks)[:, :, None], axis=1)
    outgoing = jnp.take(cache_kv, local_ids, axis=0)
    slot_count = outgoing.shape[1]
    incoming = lax.all_to_all(outgoing, "ctx", split_axis=0, concat_axis=0, tiled=True)
    incoming = incoming.reshape(ctx_count * slot_count, block_rows, kv_width)
    global_recv = from_root(cache_kv[:NG], "ctx", 0)
    remote = jnp.concatenate([window_recv, global_recv, incoming], axis=0)
    random_start = WIN + NG
    global_pos = WIN + jnp.arange(NG, dtype=jnp.int32)
    prompt_start = remote.shape[0]
    key_pool = jnp.concatenate([remote, prompt_key_value], axis=0)
    own_refs = lax.dynamic_index_in_dim(per_reader, ctx_index, 0, keepdims=False)
    own_ranks = lax.dynamic_index_in_dim(slot_rank, ctx_index, 0, keepdims=False)
    random_pos = (random_start + own_refs // cache_blocks * slot_count + own_ranks).reshape(
        local_blocks, rand_count
    )
    local_order = jnp.arange(local_blocks, dtype=jnp.int32)
    global_order = ctx_index * local_blocks + local_order
    steps_back = jnp.arange(WIN, 0, -1, dtype=jnp.int32)
    back_local = local_order[:, None] - steps_back[None, :]
    window_pos = jnp.where(back_local >= 0, prompt_start + back_local, WIN + back_local)
    back_global = global_order[:, None] - steps_back[None, :]
    positions = jnp.concatenate(
        [
            jnp.broadcast_to(global_pos[None, :], (local_blocks, NG)),
            random_pos,
            window_pos,
            (prompt_start + local_order)[:, None],
        ],
        axis=1,
    )
    block_ok = jnp.concatenate(
        [
            jnp.ones((local_blocks, NG + rand_count), dtype=bool),
            back_global >= 0,
            jnp.ones((local_blocks, 1), dtype=bool),
        ],
        axis=1,
    )
    cache_ids = jnp.concatenate(
        [
            jnp.broadcast_to(jnp.arange(NG, dtype=jnp.int32)[None, :], (local_blocks, NG)),
            own_refs.reshape(local_blocks, rand_count),
        ],
        axis=1,
    )
    prompt_ids = jnp.concatenate([jnp.maximum(back_global, 0), global_order[:, None]], axis=1)
    scale_row_table = jnp.concatenate(
        [jnp.take(cache_scale, cache_ids, axis=0), jnp.take(prompt_scale, prompt_ids, axis=0)],
        axis=1,
    )
    key_total = positions.shape[1]
    query_ids = sub_index * row_count + jnp.arange(row_count, dtype=jnp.int32)
    key_ids = jnp.arange(key_total * block_rows, dtype=jnp.int32)
    last_start = (key_total - 1) * block_rows
    causal = (key_ids[None, :] < last_start) | (key_ids[None, :] - last_start <= query_ids[:, None])

    def attend(packed):
        query_block, block_pos, usable, scale_one = packed
        collected_rows = jnp.take(key_pool, block_pos, axis=0).reshape(
            key_total * block_rows, local_heads, 2, head_dim
        )
        key_vals = collected_rows[:, :, 0]
        value_vals = collected_rows[:, :, 1]
        scale_one = scale_one.reshape(key_total, local_heads, 2)
        key_scale = jnp.repeat(scale_one[:, :, 0], block_rows, axis=0).T
        value_scale = jnp.repeat(scale_one[:, :, 1], block_rows, axis=0).T
        query_entries = query_block.reshape(row_count, local_heads, query_groups, head_dim)
        scores = jnp.einsum(
            "rhgd,khd->hgrk", query_entries, key_vals, preferred_element_type=jnp.float32
        )
        scores = scores * (key_scale / math.sqrt(head_dim))[:, None, None, :]
        allowed = causal & jnp.repeat(usable, block_rows)[None, :]
        scores = jnp.where(allowed[None, None], scores, -jnp.inf)
        row_max = jnp.max(scores, axis=-1, keepdims=True)
        probs = jnp.exp(scores - row_max)
        totals = jnp.sum(probs, axis=-1)
        weights = (probs * value_scale[:, None, None, :]).astype(jnp.bfloat16)
        result = jnp.einsum(
            "hgrk,khd->rhgd", weights, value_vals, preferred_element_type=jnp.float32
        )
        result = result / jnp.transpose(totals, (2, 0, 1))[..., None]
        return result.astype(jnp.bfloat16).reshape(row_count, query_width)

    return lax.map(attend, (queries, positions, block_ok, scale_row_table))


def solution(mesh):
    in_specs = (
        P(("group", "ctx"), "sub", "kvh"),
        P(("group", "ctx"), None, "kvh"),
        P("group", "kvh"),
        P(("group", "ctx"), None, "kvh"),
        P("group", "kvh"),
        P("group", None),
    )
    out_specs = P(("group", "ctx"), "sub", "kvh")
    return jax.shard_map(body, mesh=mesh, in_specs=in_specs, out_specs=out_specs, check_vma=False)
```

profile of v0, /device:TPU:18, one launch (start us, length us, event | category | flops | bytes accessed | tf_op | source)
XLA Modules:
  0.0 353.2 jit_solution(6143707846423039315)
XLA Ops:
  8.3 7.2 %gather_fusion.1 = bf16[24,128,1024]{2,1,0:T(8,128)(2,1)} fusion(bf16[24,128,1024]{2,1,0:T(8,128)(2,1)} %param.9, s32[1024]{0:T(1024)S(1)} %pad_clamp_fusion.3), kind=kCustom, calls=%fused_computation.1 | custom fusion | bytes 12583008 | tf_op jit(solution)/shard_map/jit(_take)/gather | solution.py:47
  15.5 6.1 %broadcast_select_fusion = bf16[4,6,128,1024]{3,2,1,0:T(8,128)(2,1)} fusion(bf16[4,6,128,1024]{3,2,1,0:T(8,128)(2,1)} %bitcast.138, pred[4,6]{1,0:T(4,128)(4,1)S(1)} %copy.33), kind=kLoop, calls=%fused_computation.43 | loop fusion | flops 3145728 | bytes 12582936 | tf_op jit(solution)/shard_map/jit(_take)/select_n | solution.py:47
  21.6 5.7 %all-to-all-start = ((bf16[4,6,128,1024]{3,2,1,0:T(8,128)(2,1)}), bf16[4,6,128,1024]{3,2,1,0:T(8,128)(2,1)}, u32[]{:S(2)}, u32[]{:S(2)}) async-start(bf16[4,6,128,1024]{3,2,1,0:T(8,128)(2,1)} %broadcast_select_fusion), calls=%async_computation | async-start | bytes 12582912 | tf_op jit(solution)/shard_map/all_to_all | solution.py:49
  29.3 3.4 collective-permute-start
  35.9 115.8 %all-reduce.2.cloned.1.call-done = bf16[2,128,1024]{2,1,0:T(8,128)(2,1)} async-done(((bf16[2,128,1024]{2,1,0:T(8,128)(2,1)}), bf16[2,128,1024]{2,1,0:T(8,128)(2,1)}) %all-reduce.2.cloned.1.call-update) | async-done | bytes 524304 | tf_op jit(solution)/shard_map/psum | solution.py:21
  151.7 39.7 %collective-permute-done = bf16[2,128,1024]{2,1,0:T(8,128)(2,1)S(1)} collective-permute-done((bf16[2,128,1024]{2,1,0:T(8,128)(2,1)S(1)}, bf16[2,128,1024]{2,1,0:T(8,128)(2,1)S(1)}, u32[]{:S(2)}, u32[]{:S(2)}) %collective-permute-start) | collective-permute-done | bytes 524320 | tf_op jit(solution)/shard_map/ppermute | solution.py:16
  191.4 6.9 %pad_maximum_fusion = bf16[36,128,1024]{2,1,0:T(8,128)(2,1)} fusion(bf16[8,128,1024]{2,1,0:T(8,128)(2,1)S(1)} %copy-done, bf16[24,128,1024]{2,1,0:T(8,128)(2,1)} %bitcast.2, bf16[2,128,1024]{2,1,0:T(8,128)(2,1)} %all-reduce.2.cloned.1.call-done, bf16[2,128,1024]{2,1,0:T(8,128)(2,1)S(1)} %collective-permute-done), kind=kLoop, calls=%fused_computation.42 | loop fusion | flops 14155776 | bytes 18874368 | tf_op jit(solution)/shard_map/concatenate | solution.py:56
  198.3 148.0 %while.11 = (s32[]{:T(128)}, bf16[8,64,4096]{2,1,0:T(8,128)(2,1)}, s32[8,8]{1,0:T(8,128)S(1)}, bf16[36,128,1024]{2,1,0:T(8,128)(2,1)}, pred[8,8]{1,0:T(8,128)(4,...) while((s32[]{:T(128)}, bf16[8,64,4096]{2,1,0:T(8,128)(2,1)}, ...), condition=%wide.region_7.8_spmd.clone, body=%wide.region_4.7_spmd.clone.sunk | while | flops 1092290688 | bytes 54828360 | solution.py:130
  198.4 5.7 %gather_fusion = bf16[8,128,1024]{2,1,0:T(8,128)(2,1)} fusion(bf16[36,128,1024]{2,1,0:T(8,128)(2,1)} %get-tuple-element.220, s32[1024]{0:T(1024)S(1)} %pad_clamp_fusion.5), kind=kCustom, calls=%fused_computation.clone.clone.1 | custom fusion | bytes 4194336 | tf_op jit(solution)/shard_map/while/body/eval_jaxpr/jit(_take)/gather | solution.py:105
  210.5 3.6 %fusion.39 = (f32[4,8,64]{2,1,0:T(8,128)S(1)}, f32[4,8,64,1024]{3,2,1,0:T(8,128)S(1)}) fusion(f32[4,1024,64,8]{1,2,3,0:T(8,128)S(1)} %fusion.37, f32[4,1024]{1,0:T(4,128)S(1)} %bitcast.141, pred[64,1024]{1,0:T(8,128)(4,1)S(1)} %or_and_fusion.2), kind=kOutput, calls=%fused_computation.100.clone.1 | output fusion | flops 12583935 | bytes 16867328 | tf_op jit(solution)/shard_map/while/body/eval_jaxpr/sub | solution.py:121
  216.9 5.7 %gather_fusion = bf16[8,128,1024]{2,1,0:T(8,128)(2,1)} fusion(bf16[36,128,1024]{2,1,0:T(8,128)(2,1)} %get-tuple-element.220, s32[1024]{0:T(1024)S(1)} %pad_clamp_fusion.5), kind=kCustom, calls=%fused_computation.clone.clone.1 | custom fusion | bytes 4194336 | tf_op jit(solution)/shard_map/while/body/eval_jaxpr/jit(_take)/gather | solution.py:105
  229.0 3.6 %fusion.39 = (f32[4,8,64]{2,1,0:T(8,128)S(1)}, f32[4,8,64,1024]{3,2,1,0:T(8,128)S(1)}) fusion(f32[4,1024,64,8]{1,2,3,0:T(8,128)S(1)} %fusion.37, f32[4,1024]{1,0:T(4,128)S(1)} %bitcast.141, pred[64,1024]{1,0:T(8,128)(4,1)S(1)} %or_and_fusion.2), kind=kOutput, calls=%fused_computation.100.clone.1 | output fusion | flops 12583935 | bytes 16867328 | tf_op jit(solution)/shard_map/while/body/eval_jaxpr/sub | solution.py:121
  235.4 5.7 %gather_fusion = bf16[8,128,1024]{2,1,0:T(8,128)(2,1)} fusion(bf16[36,128,1024]{2,1,0:T(8,128)(2,1)} %get-tuple-element.220, s32[1024]{0:T(1024)S(1)} %pad_clamp_fusion.5), kind=kCustom, calls=%fused_computation.clone.clone.1 | custom fusion | bytes 4194336 | tf_op jit(solution)/shard_map/while/body/eval_jaxpr/jit(_take)/gather | solution.py:105
  247.5 3.6 %fusion.39 = (f32[4,8,64]{2,1,0:T(8,128)S(1)}, f32[4,8,64,1024]{3,2,1,0:T(8,128)S(1)}) fusion(f32[4,1024,64,8]{1,2,3,0:T(8,128)S(1)} %fusion.37, f32[4,1024]{1,0:T(4,128)S(1)} %bitcast.141, pred[64,1024]{1,0:T(8,128)(4,1)S(1)} %or_and_fusion.2), kind=kOutput, calls=%fused_computation.100.clone.1 | output fusion | flops 12583935 | bytes 16867328 | tf_op jit(solution)/shard_map/while/body/eval_jaxpr/sub | solution.py:121
  253.9 5.7 %gather_fusion = bf16[8,128,1024]{2,1,0:T(8,128)(2,1)} fusion(bf16[36,128,1024]{2,1,0:T(8,128)(2,1)} %get-tuple-element.220, s32[1024]{0:T(1024)S(1)} %pad_clamp_fusion.5), kind=kCustom, calls=%fused_computation.clone.clone.1 | custom fusion | bytes 4194336 | tf_op jit(solution)/shard_map/while/body/eval_jaxpr/jit(_take)/gather | solution.py:105
  266.0 3.6 %fusion.39 = (f32[4,8,64]{2,1,0:T(8,128)S(1)}, f32[4,8,64,1024]{3,2,1,0:T(8,128)S(1)}) fusion(f32[4,1024,64,8]{1,2,3,0:T(8,128)S(1)} %fusion.37, f32[4,1024]{1,0:T(4,128)S(1)} %bitcast.141, pred[64,1024]{1,0:T(8,128)(4,1)S(1)} %or_and_fusion.2), kind=kOutput, calls=%fused_computation.100.clone.1 | output fusion | flops 12583935 | bytes 16867328 | tf_op jit(solution)/shard_map/while/body/eval_jaxpr/sub | solution.py:121
  272.4 5.7 %gather_fusion = bf16[8,128,1024]{2,1,0:T(8,128)(2,1)} fusion(bf16[36,128,1024]{2,1,0:T(8,128)(2,1)} %get-tuple-element.220, s32[1024]{0:T(1024)S(1)} %pad_clamp_fusion.5), kind=kCustom, calls=%fused_computation.clone.clone.1 | custom fusion | bytes 4194336 | tf_op jit(solution)/shard_map/while/body/eval_jaxpr/jit(_take)/gather | solution.py:105
  284.5 3.6 %fusion.39 = (f32[4,8,64]{2,1,0:T(8,128)S(1)}, f32[4,8,64,1024]{3,2,1,0:T(8,128)S(1)}) fusion(f32[4,1024,64,8]{1,2,3,0:T(8,128)S(1)} %fusion.37, f32[4,1024]{1,0:T(4,128)S(1)} %bitcast.141, pred[64,1024]{1,0:T(8,128)(4,1)S(1)} %or_and_fusion.2), kind=kOutput, calls=%fused_computation.100.clone.1 | output fusion | flops 12583935 | bytes 16867328 | tf_op jit(solution)/shard_map/while/body/eval_jaxpr/sub | solution.py:121
  290.9 5.7 %gather_fusion = bf16[8,128,1024]{2,1,0:T(8,128)(2,1)} fusion(bf16[36,128,1024]{2,1,0:T(8,128)(2,1)} %get-tuple-element.220, s32[1024]{0:T(1024)S(1)} %pad_clamp_fusion.5), kind=kCustom, calls=%fused_computation.clone.clone.1 | custom fusion | bytes 4194336 | tf_op jit(solution)/shard_map/while/body/eval_jaxpr/jit(_take)/gather | solution.py:105
  303.0 3.6 %fusion.39 = (f32[4,8,64]{2,1,0:T(8,128)S(1)}, f32[4,8,64,1024]{3,2,1,0:T(8,128)S(1)}) fusion(f32[4,1024,64,8]{1,2,3,0:T(8,128)S(1)} %fusion.37, f32[4,1024]{1,0:T(4,128)S(1)} %bitcast.141, pred[64,1024]{1,0:T(8,128)(4,1)S(1)} %or_and_fusion.2), kind=kOutput, calls=%fused_computation.100.clone.1 | output fusion | flops 12583935 | bytes 16867328 | tf_op jit(solution)/shard_map/while/body/eval_jaxpr/sub | solution.py:121
  309.4 5.7 %gather_fusion = bf16[8,128,1024]{2,1,0:T(8,128)(2,1)} fusion(bf16[36,128,1024]{2,1,0:T(8,128)(2,1)} %get-tuple-element.220, s32[1024]{0:T(1024)S(1)} %pad_clamp_fusion.5), kind=kCustom, calls=%fused_computation.clone.clone.1 | custom fusion | bytes 4194336 | tf_op jit(solution)/shard_map/while/body/eval_jaxpr/jit(_take)/gather | solution.py:105
  321.5 3.6 %fusion.39 = (f32[4,8,64]{2,1,0:T(8,128)S(1)}, f32[4,8,64,1024]{3,2,1,0:T(8,128)S(1)}) fusion(f32[4,1024,64,8]{1,2,3,0:T(8,128)S(1)} %fusion.37, f32[4,1024]{1,0:T(4,128)S(1)} %bitcast.141, pred[64,1024]{1,0:T(8,128)(4,1)S(1)} %or_and_fusion.2), kind=kOutput, calls=%fused_computation.100.clone.1 | output fusion | flops 12583935 | bytes 16867328 | tf_op jit(solution)/shard_map/while/body/eval_jaxpr/sub | solution.py:121
  327.9 5.7 %gather_fusion = bf16[8,128,1024]{2,1,0:T(8,128)(2,1)} fusion(bf16[36,128,1024]{2,1,0:T(8,128)(2,1)} %get-tuple-element.220, s32[1024]{0:T(1024)S(1)} %pad_clamp_fusion.5), kind=kCustom, calls=%fused_computation.clone.clone.1 | custom fusion | bytes 4194336 | tf_op jit(solution)/shard_map/while/body/eval_jaxpr/jit(_take)/gather | solution.py:105
  340.0 3.6 %fusion.39 = (f32[4,8,64]{2,1,0:T(8,128)S(1)}, f32[4,8,64,1024]{3,2,1,0:T(8,128)S(1)}) fusion(f32[4,1024,64,8]{1,2,3,0:T(8,128)S(1)} %fusion.37, f32[4,1024]{1,0:T(4,128)S(1)} %bitcast.141, pred[64,1024]{1,0:T(8,128)(4,1)S(1)} %or_and_fusion.2), kind=kOutput, calls=%fused_computation.100.clone.1 | output fusion | flops 12583935 | bytes 16867328 | tf_op jit(solution)/shard_map/while/body/eval_jaxpr/sub | solution.py:121
  (246 shorter events, 80.1 us)
Async XLA Ops:
  21.6 7.6 %copy-start = (bf16[8,128,1024]{2,1,0:T(8,128)(2,1)S(1)}, bf16[8,128,1024]{2,1,0:T(8,128)(2,1)}, u32[]{:S(2)}) copy-start(bf16[8,128,1024]{2,1,0:T(8,128)(2,1)} %param.11) | copy-start | bytes 6291460
  21.6 11.4 %copy-start.2 = (f32[96,8]{0,1:T(8,128)S(1)}, f32[96,8]{0,1:T(8,128)}, u32[]{:S(2)}) copy-start(f32[96,8]{0,1:T(8,128)} %param.10) | copy-start | bytes 9220
  21.6 12.7 %copy-start.1 = (f32[32,8]{0,1:T(8,128)S(1)}, f32[32,8]{0,1:T(8,128)}, u32[]{:S(2)}) copy-start(f32[32,8]{0,1:T(8,128)} %param.12) | copy-start | bytes 3076
  21.6 169.8 %all-to-all-start = ((bf16[4,6,128,1024]{3,2,1,0:T(8,128)(2,1)}), bf16[4,6,128,1024]{3,2,1,0:T(8,128)(2,1)}, u32[]{:S(2)}, u32[]{:S(2)}) async-start(bf16[4,6,128,1024]{3,2,1,0:T(8,128)(2,1)} %broadcast_select_fusion), calls=%async_computation | async-start | bytes 12582912 | tf_op jit(solution)/shard_map/all_to_all | solution.py:49
  27.3 124.3 %all-reduce.2.cloned.1.call-start = ((), (), s32[]{:S(2)}) async-start(), calls=%async_computation.1 | async-start | bytes 1048576 | tf_op jit(solution)/shard_map/psum | solution.py:21
  29.3 162.1 %collective-permute-start = (bf16[2,128,1024]{2,1,0:T(8,128)(2,1)S(1)}, bf16[2,128,1024]{2,1,0:T(8,128)(2,1)S(1)}, u32[]{:S(2)}, u32[]{:S(2)}) collective-permute-start(bf16[2,128,1024]{2,1,0:T(8,128)(2,1)S(1)} %slice.18), channel_id=1, source_target_pairs={{0,4},{4,8},{8,12},{1,5},{5,9},{9,13},{2,6},{6,10},{10,14},{3,7},{... | collective-permute-start | bytes 1572872 | tf_op jit(solution)/shard_map/ppermute | solution.py:16
Sparse Core Ops, SparseCore 0:
  30.5 121.1 all-reduce.1
where the time goes:
time: 355 us; the launch traced here: 353 us
  waiting for transfers between devices  156 us (44%)
  local copies, waits for them, and re-layouts  105 us (30%)
  other arithmetic  49 us (14%)
  matrix products  20.2 us (6%)
  between operations  13.5 us (4%)
  starting transfers between devices  9.08 us (3%)
    psum x1, waiting for transfers between devices, from_root(): return lax.psum(block, axis)  116 us
    gather x16, local copies, waits for them, and re-layouts, attend(): jnp.take(key_pool, block_pos, axis=0)  71.2 us
    ppermute x1, waiting for transfers between devices, passed_along(): return lax.ppermute(block, axis, route)  39.7 us
    sub x8, other arithmetic, attend(): probs = jnp.exp(scores - row_max)  28.6 us
    while x48, local copies, waits for them, and re-layouts  10.6 us
    dot_general x8, matrix products, attend(): jnp.einsum('rhgd,khd->hgrk', query_entries, key_vals, preferred_element_t...  10.2 us
    dot_general x8, matrix products, attend(): jnp.einsum('hgrk,khd->rhgd', weights, value_vals, preferred_element_type=...  10 us
    gather x1, local copies, waits for them, and re-layouts, body(): outgoing = jnp.take(cache_kv, local_ids, axis=0)  7.22 us
  transfers between devices with their start and end apart: 3, of which 2 were waited for; matrix products, arithmetic and copies ran while one was open for 1% of the time, Pallas kernels for 0%

commit v1 on v0

v1 whole, which is shorter than its diff:
```python
import functools
import math

import jax
import jax.numpy as jnp
from jax import lax
from jax.experimental import pallas as pl
from jax.experimental.pallas import tpu as pltpu
from jax.sharding import PartitionSpec as P

HEAD = 128
NG = 2
WIN = 2
FAR = -1e30
MESH = pl.DeviceIdType.MESH


def flipped(me, k):
    out, bit = me, 1
    while bit <= k:
        if k & bit:
            out = out + bit - 2 * bit * ((me // bit) % 2)
        bit *= 2
    return out


def kernel(
    n, cap, q_hbm, c_hbm, cs, p_hbm, ps, rnd, o_hbm,
    qbuf, cbuf, pk, gbuf, pool, outb, obuf, acc1, m1, l1, bias, places,
    loc, osem, rs, rr, fs, fr, gs, gr, gfs, gfr, ws, wr, wfs, wfr,
):
    nq, rows, width = q_hbm.shape
    nc, block, kvw = c_hbm.shape
    heads = kvw // (2 * HEAD)
    groups = width // (heads * HEAD)
    lanes = groups * rows
    half = block // 2
    rand = rnd.shape[1]
    me, sub = lax.axis_index("ctx"), lax.axis_index("sub")
    other = 1 - sub
    mine = pl.ds(pl.multiple_of(sub * half, half), half)
    theirs = pl.ds(pl.multiple_of(other * half, half), half)
    order = range(n - 1, 0, -1)

    local_p = pltpu.make_async_copy(p_hbm, pk.at[pl.ds(WIN, nq)], loc.at[0])
    local_c = pltpu.make_async_copy(c_hbm, cbuf, loc.at[1])
    local_q = pltpu.make_async_copy(q_hbm, qbuf, loc.at[2])
    local_g = pltpu.make_async_copy(c_hbm.at[pl.ds(0, NG)], gbuf, loc.at[3])

    @pl.when(me == 0)
    def _():
        local_g.start()

    local_p.start()
    local_c.start()
    local_q.start()

    barrier = pltpu.get_barrier_semaphore()
    for k in order:
        pl.semaphore_signal(barrier, inc=1, device_id={"ctx": flipped(me, k)}, device_id_type=MESH)
    pl.semaphore_signal(barrier, inc=1, device_id={"sub": other}, device_id_type=MESH)
    pl.semaphore_wait(barrier, n)

    def remote(src, dst, send, recv, where):
        return pltpu.make_async_remote_copy(
            src_ref=src, dst_ref=dst, send_sem=send, recv_sem=recv,
            device_id=where, device_id_type=MESH,
        )

    onward = {"ctx": lax.rem(me + 1, n)}
    sibling = {"sub": other}
    send_g = remote(gbuf.at[:, mine], gbuf.at[:, mine], gs, gr, onward)
    share_g = remote(gbuf.at[:, mine], gbuf.at[:, mine], gfs, gfr, sibling)
    heard_g = remote(gbuf.at[:, theirs], gbuf.at[:, theirs], gfs, gfr, sibling)
    send_w = remote(pk.at[pl.ds(nq, WIN), mine], pk.at[pl.ds(0, WIN), mine], ws, wr, onward)
    share_w = remote(pk.at[pl.ds(0, WIN), mine], pk.at[pl.ds(0, WIN), mine], wfs, wfr, sibling)
    heard_w = remote(pk.at[pl.ds(0, WIN), theirs], pk.at[pl.ds(0, WIN), theirs], wfs, wfr, sibling)

    def run(owner, side):
        return pool.at[pl.ds((owner * 2 + side) * cap, cap)]

    def send_r(k):
        return remote(outb.at[k - 1], run(me, sub), rs.at[k - 1], rr.at[k - 1], {"ctx": flipped(me, k)})

    def came_r(k):
        mate = flipped(me, k)
        return remote(outb.at[k - 1], run(mate, sub), rs.at[k - 1], rr.at[k - 1], {"ctx": mate})

    def share_r(k):
        part = run(flipped(me, k), sub)
        return remote(part, part, fs.at[k - 1], fr.at[k - 1], sibling)

    def heard_r(k):
        part = run(flipped(me, k), other)
        return remote(part, part, fs.at[k - 1], fr.at[k - 1], sibling)

    @pl.when(me == 0)
    def _():
        local_g.wait()
        send_g.start()

    local_p.wait()

    @pl.when(me < n - 1)
    def _():
        send_w.start()

    local_c.wait()

    def picks(reader):
        def step(b, carry):
            count, slots = carry[0], list(carry[1:])
            for r in range(rand):
                ref = rnd[reader * nq + b, r]
                own = lax.div(ref, nc) == me
                for j in range(cap):
                    slots[j] = jnp.where(own & (count == j), ref - me * nc, slots[j])
                count = count + own.astype(jnp.int32)
            return (count, *slots)

        zero = jnp.int32(0)
        return lax.fori_loop(0, nq, step, (zero,) * (cap + 1))[1:]

    for k in order:
        for j, slot in enumerate(picks(flipped(me, k))):
            outb[k - 1, j] = cbuf[slot, mine, :]
        send_r(k).start()
    for j, slot in enumerate(picks(me)):
        for side in range(2):
            pool[(me * 2 + side) * cap + j] = cbuf[slot, pl.ds(side * half, half), :]

    def place(i, _):
        ref = rnd[me * nq + i // rand, i % rand]
        owner = lax.div(ref, nc)

        def earlier(j, count):
            same = lax.div(rnd[me * nq + j // rand, j % rand], nc) == owner
            return count + same.astype(jnp.int32)

        places[i] = owner * (2 * cap) + lax.fori_loop(0, i, earlier, jnp.int32(0))
        return 0

    lax.fori_loop(0, nq * rand, place, 0)
    key_row = lax.broadcasted_iota(jnp.int32, (block, lanes), 0)
    query_row = lax.broadcasted_iota(jnp.int32, (block, lanes), 1) % rows + sub * rows
    bias[...] = jnp.where(key_row <= query_row, 0.0, FAR).astype(jnp.float32)

    @pl.when(me > 0)
    def _():
        send_g.wait_recv()
        share_g.start()

        @pl.when(me < n - 1)
        def _():
            send_g.start()

        send_w.wait_recv()
        share_w.start()
        heard_g.wait_recv()
        heard_w.wait_recv()

    @pl.when(me == 0)
    def _():
        pk[pl.ds(0, WIN)] = jnp.zeros((WIN, block, kvw), pk.dtype)

    local_q.wait()
    unit = math.log2(math.e) / math.sqrt(HEAD)

    def head_queries(b, h):
        at = h * groups * HEAD
        return jnp.concatenate(
            [qbuf[b, :, at + g * HEAD : at + (g + 1) * HEAD] for g in range(groups)], axis=0
        )

    def columns(h, value):
        return slice((2 * h + value) * HEAD, (2 * h + value + 1) * HEAD)

    def part(q, keys, values, scales, masked, carry):
        st = lax.dot_general(
            jnp.concatenate(keys, axis=0), q, (((1,), (1,)), ((), ())),
            preferred_element_type=jnp.float32,
        )
        pieces = [st[j * block : (j + 1) * block] for j in range(len(scales))]
        if masked:
            pieces[-1] = pieces[-1] + bias[...]
        tops = [
            jnp.max(piece, axis=0, keepdims=True) * c + off
            for piece, (c, _, off) in zip(pieces, scales)
        ]
        top = functools.reduce(jnp.maximum, tops)
        if carry is not None:
            top = jnp.maximum(top, carry[0])
        total, weights = 0.0, []
        for piece, (c, v, off) in zip(pieces, scales):
            v = jnp.full((1, lanes), v, jnp.float32)
            w = jnp.exp2(piece * c - (top - off - jnp.log2(v)))
            total = total + jnp.sum(w, axis=0, keepdims=True) / v
            weights.append(w.astype(jnp.bfloat16))
        acc = lax.dot_general(
            jnp.concatenate(values, axis=0), jnp.concatenate(weights, axis=0),
            (((0,), (0,)), ((), ())), preferred_element_type=jnp.float32,
        )
        if carry is not None:
            fade = jnp.exp2(carry[0] - top)
            total = total + carry[1] * fade
            acc = acc + carry[2] * fade
        return top, total, acc

    def near(b, _):
        at = me * nq + b
        for h in range(heads):
            q = head_queries(b, h)
            keys, values = [], []
            for value, into in ((0, keys), (1, values)):
                cols = columns(h, value)
                into += [gbuf[j, :, cols] for j in range(NG)]
                into += [pk[b + j, :, cols] for j in range(WIN + 1)]
            scales = [(cs[j, 2 * h] * unit, cs[j, 2 * h + 1], 0.0) for j in range(NG)]
            for j in range(WIN, 0, -1):
                there = at >= j
                row = jnp.maximum(at - j, 0)
                c = jnp.where(there, ps[row, 2 * h] * unit, 0.0)
                scales.append((c, ps[row, 2 * h + 1], jnp.where(there, 0.0, FAR)))
            scales.append((ps[at, 2 * h] * unit, ps[at, 2 * h + 1], 0.0))
            m1[b, h], l1[b, h], acc1[b, h] = part(q, keys, values, scales, True, None)
        return 0

    lax.fori_loop(0, nq, near, 0)

    for k in reversed(order):
        came_r(k).wait_recv()
        share_r(k).start()
    for k in order:
        heard_r(k).wait_recv()

    def far(b, _):
        spots = [places[b * rand + r] for r in range(rand)]
        refs = [rnd[me * nq + b, r] for r in range(rand)]
        for h in range(heads):
            q = head_queries(b, h)
            keys, values = [], []
            for value, into in ((0, keys), (1, values)):
                cols = columns(h, value)
                for spot in spots:
                    into += [pool[spot, :, cols], pool[spot + cap, :, cols]]
            scales = [(cs[ref, 2 * h] * unit, cs[ref, 2 * h + 1], 0.0) for ref in refs]
            carry = (m1[b, h], l1[b, h], acc1[b, h])
            _, total, acc = part(q, keys, values, scales, False, carry)
            out = jnp.transpose(acc / total).astype(jnp.bfloat16)
            at = h * groups * HEAD
            for g in range(groups):
                obuf[b, :, at + g * HEAD : at + (g + 1) * HEAD] = out[g * rows : (g + 1) * rows]
        pltpu.make_async_copy(obuf.at[b], o_hbm.at[b], osem.at[b]).start()
        return 0

    lax.fori_loop(0, nq, far, 0)

    for b in range(nq):
        pltpu.make_async_copy(obuf.at[b], o_hbm.at[b], osem.at[b]).wait()

    @pl.when(me < n - 1)
    def _():
        send_g.wait_send()
        send_w.wait_send()

    @pl.when(me > 0)
    def _():
        share_g.wait_send()
        share_w.wait_send()

    for k in order:
        send_r(k).wait_send()
        share_r(k).wait_send()


def body(queries, cache_kv, cache_scale, prompt_key_value, prompt_scale, rand_blocks):
    n = lax.axis_size("ctx")
    nq, rows, width = queries.shape
    nc, block, kvw = cache_kv.shape
    rand = rand_blocks.shape[1]
    cap = max(2, (nq * rand + n - 1) // n)
    heads = kvw // (2 * HEAD)
    lanes = width // (heads * HEAD) * rows
    half = block // 2
    bf, f32 = jnp.bfloat16, jnp.float32
    hbm = pl.BlockSpec(memory_space=pl.ANY)
    smem = pl.BlockSpec(memory_space=pltpu.SMEM)
    dma = pltpu.SemaphoreType.DMA
    keys = (NG + rand + WIN + 1) * block
    return pl.pallas_call(
        functools.partial(kernel, n, cap),
        out_shape=jax.ShapeDtypeStruct(queries.shape, bf),
        in_specs=[hbm, hbm, smem, hbm, smem, smem],
        out_specs=hbm,
        scratch_shapes=[
            pltpu.VMEM((nq, rows, width), bf),
            pltpu.VMEM((nc, block, kvw), bf),
            pltpu.VMEM((WIN + nq, block, kvw), bf),
            pltpu.VMEM((NG, block, kvw), bf),
            pltpu.VMEM((n * 2 * cap, half, kvw), bf),
            pltpu.VMEM((n - 1, cap, half, kvw), bf),
            pltpu.VMEM((nq, rows, width), bf),
            pltpu.VMEM((nq, heads, HEAD, lanes), f32),
            pltpu.VMEM((nq, heads, 1, lanes), f32),
            pltpu.VMEM((nq, heads, 1, lanes), f32),
            pltpu.VMEM((block, lanes), f32),
            pltpu.SMEM((nq * rand,), jnp.int32),
            dma((4,)), dma((nq,)),
            dma((n - 1,)), dma((n - 1,)), dma((n - 1,)), dma((n - 1,)),
            dma, dma, dma, dma, dma, dma, dma, dma,
        ],
        compiler_params=pltpu.CompilerParams(
            collective_id=0, has_side_effects=True, vmem_limit_bytes=56 * 2**20
        ),
        cost_estimate=pl.CostEstimate(
            flops=4 * nq * width * rows * keys,
            bytes_accessed=2 * nc * block * kvw + 4 * nq * rows * width,
            transcendentals=nq * heads * lanes * keys,
        ),
    )(queries, cache_kv, cache_scale, prompt_key_value, prompt_scale, rand_blocks)


def solution(mesh):
    in_specs = (
        P(("group", "ctx"), "sub", "kvh"),
        P(("group", "ctx"), None, "kvh"),
        P("group", "kvh"),
        P(("group", "ctx"), None, "kvh"),
        P("group", "kvh"),
        P("group", None),
    )
    out_specs = P(("group", "ctx"), "sub", "kvh")
    return jax.shard_map(body, mesh=mesh, in_specs=in_specs, out_specs=out_specs, check_vma=False)
```

time: 355 us -> 143 us (0.40)
  the two profiles are of different devices: /device:TPU:18 before, /device:TPU:24 now
where the time goes in v1:
time: 143 us
  Pallas kernels  134 us (94%)
  local copies, waits for them, and re-layouts  8.81 us (6%)
    pallas_call x1, Pallas kernels, body(): pl.pallas_call(functools.partial(kernel, n, cap), out_shape=jax.ShapeDtyp...  134 us
    unnamed x4, local copies, waits for them, and re-layouts  8.81 us

profile of v1, /device:TPU:24, one launch (start us, length us, event | category | flops | bytes accessed | tf_op | source)
XLA Modules:
  0.0 142.9 jit_solution(5931548169381337871)
XLA Ops:
  0.0 1.4 copy.8.ps
  1.4 1.4 copy.9.rnd
  2.7 1.4 copy.7.cs
  4.1 134.0 %shard_map.64 = bf16[8,64,4096]{2,1,0:T(8,128)(2,1)} custom-call(bf16[8,64,4096]{2,1,0:T(8,128)(2,1)} %q_hbm.1, bf16[24,128,1024]{2,1,0:T(8,128)(2,1)} %c_hbm.1, f32[96,8]{1,0:T(8,128)} %copy.7.cs, bf16[8,128,1024]{2,1,0:T(8,128)(2,1)} %p_hbm.1, f32[32,8]{1,0:T(8,128)} %copy.8.ps, s32[32,3]{1,0:T(8,128)} %copy.9.rnd), custom_call_target="tpu_custom_call" | custom-call | flops 8589934592 | bytes 14680064 | tf_op jit(solution)/shard_map/pallas_call | solution.py:290
  138.2 4.7 %copy.11 = bf16[8,64,4096]{2,1,0:T(8,128)(2,1)} copy(bf16[8,64,4096]{2,1,0:T(8,128)(2,1)} %shard_map.64) | data formatting | bytes 8388608

commit v2 on v1

--- a/solution.py
+++ b/solution.py
@@ -25,8 +25,8 @@
 
 
 def kernel(
-    n, cap, q_hbm, c_hbm, cs, p_hbm, ps, rnd, o_hbm,
-    qbuf, cbuf, pk, gbuf, pool, outb, obuf, acc1, m1, l1, bias, places,
+    n, cap, q_hbm, c_hbm, cs_hbm, p_hbm, ps_hbm, rnd_hbm, o_hbm,
+    qbuf, cbuf, pk, gbuf, pools, outb, obuf, acc1, m1, l1, bias, places, cs, ps, rnd,
     loc, osem, rs, rr, fs, fr, gs, gr, gfs, gfr, ws, wr, wfs, wfr,
 ):
     nq, rows, width = q_hbm.shape
@@ -35,7 +35,9 @@
     groups = width // (heads * HEAD)
     lanes = groups * rows
     half = block // 2
-    rand = rnd.shape[1]
+    rand = rnd.shape[0]
+    pair = 2 * HEAD
+    middle = n // 2
     me, sub = lax.axis_index("ctx"), lax.axis_index("sub")
     other = 1 - sub
     mine = pl.ds(pl.multiple_of(sub * half, half), half)
@@ -53,7 +55,12 @@
 
     local_p.start()
     local_c.start()
-    local_q.start()
+    tables = [
+        pltpu.make_async_copy(a, b, loc.at[4 + i])
+        for i, (a, b) in enumerate(((rnd_hbm, rnd), (cs_hbm, cs), (ps_hbm, ps)))
+    ]
+    for table in tables:
+        table.start()
 
     barrier = pltpu.get_barrier_semaphore()
     for k in order:
@@ -68,36 +75,43 @@
         )
 
     onward = {"ctx": lax.rem(me + 1, n)}
+    across = {"ctx": lax.rem(me + middle, n)}
     sibling = {"sub": other}
-    send_g = remote(gbuf.at[:, mine], gbuf.at[:, mine], gs, gr, onward)
+    send_g = remote(gbuf.at[:, mine], gbuf.at[:, mine], gs.at[0], gr, onward)
+    jump_g = remote(gbuf.at[:, mine], gbuf.at[:, mine], gs.at[1], gr, across)
     share_g = remote(gbuf.at[:, mine], gbuf.at[:, mine], gfs, gfr, sibling)
     heard_g = remote(gbuf.at[:, theirs], gbuf.at[:, theirs], gfs, gfr, sibling)
     send_w = remote(pk.at[pl.ds(nq, WIN), mine], pk.at[pl.ds(0, WIN), mine], ws, wr, onward)
     share_w = remote(pk.at[pl.ds(0, WIN), mine], pk.at[pl.ds(0, WIN), mine], wfs, wfr, sibling)
     heard_w = remote(pk.at[pl.ds(0, WIN), theirs], pk.at[pl.ds(0, WIN), theirs], wfs, wfr, sibling)
 
-    def run(owner, side):
-        return pool.at[pl.ds((owner * 2 + side) * cap, cap)]
-
-    def send_r(k):
-        return remote(outb.at[k - 1], run(me, sub), rs.at[k - 1], rr.at[k - 1], {"ctx": flipped(me, k)})
-
-    def came_r(k):
-        mate = flipped(me, k)
-        return remote(outb.at[k - 1], run(mate, sub), rs.at[k - 1], rr.at[k - 1], {"ctx": mate})
-
-    def share_r(k):
-        part = run(flipped(me, k), sub)
-        return remote(part, part, fs.at[k - 1], fr.at[k - 1], sibling)
-
-    def heard_r(k):
-        part = run(flipped(me, k), other)
-        return remote(part, part, fs.at[k - 1], fr.at[k - 1], sibling)
+    def run(h, owner, side):
+        return pools[h].at[pl.ds((owner * 2 + side) * cap, cap)]
+
+    def send_r(k, h):
+        at, mate = (k - 1, h), flipped(me, k)
+        return remote(outb.at[at], run(h, me, sub), rs.at[at], rr.at[at], {"ctx": mate})
+
+    def came_r(k, h):
+        at, mate = (k - 1, h), flipped(me, k)
+        return remote(outb.at[at], run(h, mate, sub), rs.at[at], rr.at[at], {"ctx": mate})
+
+    def share_r(k, h):
+        at, part = (k - 1, h), run(h, flipped(me, k), sub)
+        return remote(part, part, fs.at[at], fr.at[at], sibling)
+
+    def heard_r(k, h):
+        at, part = (k - 1, h), run(h, flipped(me, k), other)
+        return remote(part, part, fs.at[at], fr.at[at], sibling)
+
+    passes = (me > 0) & (me + 1 < n) & (lax.rem(me + 1, n) != middle)
 
     @pl.when(me == 0)
     def _():
         local_g.wait()
-        send_g.start()
+        jump_g.start()
+        if middle > 1:
+            send_g.start()
 
     local_p.wait()
 
@@ -106,12 +120,15 @@
         send_w.start()
 
     local_c.wait()
+    local_q.start()
+    for table in tables:
+        table.wait()
 
     def picks(reader):
         def step(b, carry):
             count, slots = carry[0], list(carry[1:])
             for r in range(rand):
-                ref = rnd[reader * nq + b, r]
+                ref = rnd[r, reader * nq + b]
                 own = lax.div(ref, nc) == me
                 for j in range(cap):
                     slots[j] = jnp.where(own & (count == j), ref - me * nc, slots[j])
@@ -123,18 +140,25 @@
 
     for k in order:
         for j, slot in enumerate(picks(flipped(me, k))):
-            outb[k - 1, j] = cbuf[slot, mine, :]
-        send_r(k).start()
+            for h in range(heads):
+                outb[k - 1, h, j] = cbuf[slot, mine, h * pair : (h + 1) * pair]
+        send_r(k, 0).start()
+    if heads > 1:
+        for k in order:
+            send_r(k, 1).start()
     for j, slot in enumerate(picks(me)):
         for side in range(2):
-            pool[(me * 2 + side) * cap + j] = cbuf[slot, pl.ds(side * half, half), :]
+            for h in range(heads):
+                pools[h][(me * 2 + side) * cap + j] = cbuf[
+                    slot, pl.ds(side * half, half), h * pair : (h + 1) * pair
+                ]
 
     def place(i, _):
-        ref = rnd[me * nq + i // rand, i % rand]
+        ref = rnd[i % rand, me * nq + i // rand]
         owner = lax.div(ref, nc)
 
         def earlier(j, count):
-            same = lax.div(rnd[me * nq + j // rand, j % rand], nc) == owner
+            same = lax.div(rnd[j % rand, me * nq + j // rand], nc) == owner
             return count + same.astype(jnp.int32)
 
         places[i] = owner * (2 * cap) + lax.fori_loop(0, i, earlier, jnp.int32(0))
@@ -148,14 +172,23 @@
     @pl.when(me > 0)
     def _():
         send_g.wait_recv()
+
+    @pl.when(passes)
+    def _():
+        send_g.start()
+
+    @pl.when(me > 0)
+    def _():
         share_g.start()
-
-        @pl.when(me < n - 1)
-        def _():
-            send_g.start()
-
         send_w.wait_recv()
         share_w.start()
+
+    for h in range(2, heads):
+        for k in order:
+            send_r(k, h).start()
+
+    @pl.when(me > 0)
+    def _():
         heard_g.wait_recv()
         heard_w.wait_recv()
 
@@ -215,52 +248,71 @@
                 cols = columns(h, value)
                 into += [gbuf[j, :, cols] for j in range(NG)]
                 into += [pk[b + j, :, cols] for j in range(WIN + 1)]
-            scales = [(cs[j, 2 * h] * unit, cs[j, 2 * h + 1], 0.0) for j in range(NG)]
+            scales = [(cs[2 * h, j] * unit, cs[2 * h + 1, j], 0.0) for j in range(NG)]
             for j in range(WIN, 0, -1):
                 there = at >= j
                 row = jnp.maximum(at - j, 0)
-                c = jnp.where(there, ps[row, 2 * h] * unit, 0.0)
-                scales.append((c, ps[row, 2 * h + 1], jnp.where(there, 0.0, FAR)))
-            scales.append((ps[at, 2 * h] * unit, ps[at, 2 * h + 1], 0.0))
+                c = jnp.where(there, ps[2 * h, row] * unit, 0.0)
+                scales.append((c, ps[2 * h + 1, row], jnp.where(there, 0.0, FAR)))
+            scales.append((ps[2 * h, at] * unit, ps[2 * h + 1, at], 0.0))
             m1[b, h], l1[b, h], acc1[b, h] = part(q, keys, values, scales, True, None)
         return 0
 
     lax.fori_loop(0, nq, near, 0)
 
-    for k in reversed(order):
-        came_r(k).wait_recv()
-        share_r(k).start()
-    for k in order:
-        heard_r(k).wait_recv()
-
-    def far(b, _):
+    def far(h, b):
         spots = [places[b * rand + r] for r in range(rand)]
-        refs = [rnd[me * nq + b, r] for r in range(rand)]
-        for h in range(heads):
-            q = head_queries(b, h)
-            keys, values = [], []
-            for value, into in ((0, keys), (1, values)):
-                cols = columns(h, value)
-                for spot in spots:
-                    into += [pool[spot, :, cols], pool[spot + cap, :, cols]]
-            scales = [(cs[ref, 2 * h] * unit, cs[ref, 2 * h + 1], 0.0) for ref in refs]
-            carry = (m1[b, h], l1[b, h], acc1[b, h])
-            _, total, acc = part(q, keys, values, scales, False, carry)
-            out = jnp.transpose(acc / total).astype(jnp.bfloat16)
-            at = h * groups * HEAD
-            for g in range(groups):
-                obuf[b, :, at + g * HEAD : at + (g + 1) * HEAD] = out[g * rows : (g + 1) * rows]
-        pltpu.make_async_copy(obuf.at[b], o_hbm.at[b], osem.at[b]).start()
-        return 0
-
-    lax.fori_loop(0, nq, far, 0)
-
-    for b in range(nq):
-        pltpu.make_async_copy(obuf.at[b], o_hbm.at[b], osem.at[b]).wait()
+        refs = [rnd[r, me * nq + b] for r in range(rand)]
+        q = head_queries(b, h)
+        keys, values = [], []
+        for value, into in ((0, keys), (1, values)):
+            cols = slice(value * HEAD, (value + 1) * HEAD)
+            for spot in spots:
+                into += [pools[h][spot, :, cols], pools[h][spot + cap, :, cols]]
+        scales = [(cs[2 * h, ref] * unit, cs[2 * h + 1, ref], 0.0) for ref in refs]
+        carry = (m1[b, h], l1[b, h], acc1[b, h])
+        _, total, acc = part(q, keys, values, scales, False, carry)
+        out = jnp.transpose(acc / total).astype(jnp.bfloat16)
+        at = h * groups * HEAD
+        for g in range(groups):
+            obuf[b, :, at + g * HEAD : at + (g + 1) * HEAD] = out[g * rows : (g + 1) * rows]
+
+    span = groups * HEAD
+    written = [
+        pltpu.make_async_copy(
+            obuf.at[:, :, pl.ds(h * span, span)], o_hbm.at[:, :, pl.ds(h * span, span)], osem.at[h]
+        )
+        for h in range(heads)
+    ]
+    together = 4 if nq % 4 == 0 else 1
+    for h in range(heads):
+        for k in reversed(order):
+            came_r(k, h).wait_recv()
+            share_r(k, h).start()
+        for k in reversed(order):
+            heard_r(k, h).wait_recv()
+
+        def several(i, _):
+            for j in range(together):
+                far(h, i * together + j)
+            return 0
+
+        lax.fori_loop(0, nq // together, several, 0)
+        written[h].start()
+
+    for copy in written:
+        copy.wait()
+
+    @pl.when(me == 0)
+    def _():
+        jump_g.wait_send()
+
+    @pl.when(passes | ((me == 0) & (middle > 1)))
+    def _():
+        send_g.wait_send()
 
     @pl.when(me < n - 1)
     def _():
-        send_g.wait_send()
         send_w.wait_send()
 
     @pl.when(me > 0)
@@ -269,8 +321,9 @@
         share_w.wait_send()
 
     for k in order:
-        send_r(k).wait_send()
-        share_r(k).wait_send()
+        for h in range(heads):
+            send_r(k, h).wait_send()
+            share_r(k, h).wait_send()
 
 
 def body(queries, cache_kv, cache_scale, prompt_key_value, prompt_scale, rand_blocks):
@@ -284,30 +337,33 @@
     half = block // 2
     bf, f32 = jnp.bfloat16, jnp.float32
     hbm = pl.BlockSpec(memory_space=pl.ANY)
-    smem = pl.BlockSpec(memory_space=pltpu.SMEM)
     dma = pltpu.SemaphoreType.DMA
+    grid = (n - 1, heads)
     keys = (NG + rand + WIN + 1) * block
     return pl.pallas_call(
         functools.partial(kernel, n, cap),
         out_shape=jax.ShapeDtypeStruct(queries.shape, bf),
-        in_specs=[hbm, hbm, smem, hbm, smem, smem],
+        in_specs=[hbm] * 6,
         out_specs=hbm,
         scratch_shapes=[
             pltpu.VMEM((nq, rows, width), bf),
             pltpu.VMEM((nc, block, kvw), bf),
             pltpu.VMEM((WIN + nq, block, kvw), bf),
             pltpu.VMEM((NG, block, kvw), bf),
-            pltpu.VMEM((n * 2 * cap, half, kvw), bf),
-            pltpu.VMEM((n - 1, cap, half, kvw), bf),
+            [pltpu.VMEM((n * 2 * cap, half, 2 * HEAD), bf)] * heads,
+            pltpu.VMEM((n - 1, heads, cap, half, 2 * HEAD), bf),
             pltpu.VMEM((nq, rows, width), bf),
             pltpu.VMEM((nq, heads, HEAD, lanes), f32),
             pltpu.VMEM((nq, heads, 1, lanes), f32),
             pltpu.VMEM((nq, heads, 1, lanes), f32),
             pltpu.VMEM((block, lanes), f32),
             pltpu.SMEM((nq * rand,), jnp.int32),
-            dma((4,)), dma((nq,)),
-            dma((n - 1,)), dma((n - 1,)), dma((n - 1,)), dma((n - 1,)),
-            dma, dma, dma, dma, dma, dma, dma, dma,
+            pltpu.SMEM(cache_scale.shape[::-1], f32),
+            pltpu.SMEM(prompt_scale.shape[::-1], f32),
+            pltpu.SMEM(rand_blocks.shape[::-1], jnp.int32),
+            dma((7,)), dma((heads,)),
+            dma(grid), dma(grid), dma(grid), dma(grid),
+            dma((2,)), dma, dma, dma, dma, dma, dma, dma,
         ],
         compiler_params=pltpu.CompilerParams(
             collective_id=0, has_side_effects=True, vmem_limit_bytes=56 * 2**20
@@ -317,7 +373,7 @@
             bytes_accessed=2 * nc * block * kvw + 4 * nq * rows * width,
             transcendentals=nq * heads * lanes * keys,
         ),
-    )(queries, cache_kv, cache_scale, prompt_key_value, prompt_scale, rand_blocks)
+    )(queries, cache_kv, cache_scale.T, prompt_key_value, prompt_scale.T, rand_blocks.T)
 
 
 def solution(mesh):

time: 143 us -> 94.4 us (0.66); the launches traced: 143 us -> 92.7 us
  Pallas kernels: 134 us -> 88 us
  local copies, waits for them, and re-layouts: 8.81 us -> 4.7 us
    pallas_call x1, Pallas kernels: 134 us -> 88 us  [body(): pl.pallas_call(functools.partial(kernel, n, cap), out_shape=jax.ShapeDtyp...]
    unnamed x4 -> x1, local copies, waits for them, and re-layouts: 8.81 us -> 4.7 us
where the time goes in v2:
time: 94.4 us; the launch traced here: 92.7 us
  Pallas kernels  88 us (93%)
  local copies, waits for them, and re-layouts  4.7 us (5%)
    pallas_call x1, Pallas kernels, body(): pl.pallas_call(functools.partial(kernel, n, cap), out_shape=jax.ShapeDtyp...  88 us
    unnamed x1, local copies, waits for them, and re-layouts  4.7 us

profile of v2, /device:TPU:24, one launch (start us, length us, event | category | flops | bytes accessed | tf_op | source)
XLA Modules:
  0.0 92.7 jit_solution(5264772525160914428)
XLA Ops:
  0.0 88.0 %shard_map.64 = bf16[8,64,4096]{2,1,0:T(8,128)(2,1)} custom-call(bf16[8,64,4096]{2,1,0:T(8,128)(2,1)} %q_hbm.1, bf16[24,128,1024]{2,1,0:T(8,128)(2,1)} %c_hbm.1, f32[8,96]{1,0:T(8,128)} %bitcast.3, bf16[8,128,1024]{2,1,0:T(8,128)(2,1)} %p_hbm.1, f32[8,32]{1,0:T(8,128)} %bitcast.4, s32[3,32]{1,0:T(4,128)} %bitcast.5), custom_call_target="tpu_custom_call" | custom-call | flops 8589934592 | bytes 14680064 | tf_op jit(solution)/shard_map/pallas_call | solution.py:343
  88.0 4.7 %copy.8 = bf16[8,64,4096]{2,1,0:T(8,128)(2,1)} copy(bf16[8,64,4096]{2,1,0:T(8,128)(2,1)} %shard_map.64) | data formatting | bytes 8388608
